TPU v7x, 256 devices: a whole 4x4x8 slice. The times are simulated.
256 devices in a mesh: dp: 4 (over y), ctx: 64 (over z, x, core).
Axes of the slice: x: 4, y: 4, z: 8, core: 2. Of those that a mesh axis runs over, the one named last changes fastest.
Arguments:
- queries: bfloat16 [4, 8192, 768], P('dp', 'ctx'), may hold values from -6 to 6
- keys: bfloat16 [4, 8192, 768], P('dp', 'ctx'), may hold values from -6 to 6
- values: bfloat16 [4, 8192, 768], P('dp', 'ctx'), may hold values from -6 to 6
- out_grad: bfloat16 [4, 8192, 768], P('dp', 'ctx'), may hold values from -6 to 6
- picks: int32 [4, 128, 16], P('dp', 'ctx'), may hold values from 0 to 127, as said below
- conv_in: bfloat16 [4, 8192, 768], P('dp', 'ctx'), may hold values from -6 to 6
- conv_weight: float32 [31, 768], replicated, may hold values from -1 to 1
- conv_grad: bfloat16 [4, 8192, 768], P('dp', 'ctx'), may hold values from -16 to 16
Outputs:
- attention: bfloat16 [4, 8192, 768], P('dp', 'ctx')
- query_grad: bfloat16 [4, 8192, 768], P('dp', 'ctx')
- key_grad: bfloat16 [4, 8192, 768], P('dp', 'ctx')
- value_grad: bfloat16 [4, 8192, 768], P('dp', 'ctx')
- conv_out: bfloat16 [4, 8192, 768], P('dp', 'ctx')
- conv_in_grad: bfloat16 [4, 8192, 768], P('dp', 'ctx')
- weight_grad: float32 [31, 768], P(None, 'ctx')
Inputs may be any that keep to these rules, and one draw needn't show every extreme that they name: picks[r, b, 0] = b; the other entries of a row are distinct and differ from b. Block c belongs to device c // 2 of ctx. The rows of one device's 2 query blocks name, from each other device, at most 1 distinct blocks, and some device names exactly 1 from some other device.
All inputs are finite; a program needn't handle non-finite values.
Results may differ from a plain program's by a relative error of at most 0.025.
Values may be sent and summed in bfloat16 or wider, within the bound.
No kernel may reach another device: no remote copies, remote signals or barrier semaphores. Data moves between devices by JAX's collectives and lax.ppermute only.
A program may use at most 192 MiB of HBM per device.

v0:
```python
import functools
import math

import jax
import jax.numpy as jnp
from jax import lax
from jax.experimental import pallas as pl
from jax.experimental.pallas import tpu as pltpu
from jax.sharding import PartitionSpec as P

Z, X, CORES = 8, 4, 2
CHIPS = Z * X
BLOCK = 64
HEAD_DIM = 64
LANES = 128
SEL = 16
KERNEL = 31
ROWS = 4 * BLOCK
HALF_INNER = 384
PAIRS = HALF_INNER // LANES
EXTRA = 16
CHUNK = 256
FIRST = 3
GATHERED = [(0, 0), (1, 0), (0, 1), (1, 1)]
PASSED = [(0, 2), (1, 2)]
TABLE, RING = (0, 1), (2,)
TAPS = KERNEL + 1
CHANNELS = 768
WIDTH = CHANNELS // (Z * X * CORES)
TAIL = 32
KEPT = ROWS - TAIL
SENT = ROWS + EXTRA + TAIL
F32, BF16 = jnp.float32, jnp.bfloat16


def index_of(z, x, core):
    return (z * X + x) * CORES + core


PLACES = [(z, x, c) for z in range(Z) for x in range(X) for c in range(CORES)]


def along(axis, shift):
    if axis == "z":
        return [(index_of(z, x, c), index_of((z + shift) % Z, x, c)) for z, x, c in PLACES]
    return [(index_of(z, x, c), index_of(z, (x + shift) % X, c)) for z, x, c in PLACES]


def move(value, axis, shift):
    return lax.ppermute(value, "ctx", along(axis, shift))


COLUMNS = [[index_of(z, x, c) for z in range(Z)] for x in range(X) for c in range(CORES)]


def after(value, *others):
    return lax.optimization_barrier((value, *others))[0]


def swap_cores(value):
    return lax.ppermute(value, "ctx", [(i, i ^ 1) for i in range(CHIPS * CORES)])


def plus(a, b):
    return (a.astype(F32) + b.astype(F32)).astype(BF16)


def scatter_across(parts, far_up, far_down):
    cut = far_up.shape[0]
    above, below = parts[1], parts[3]
    up, down = move(far_up, "x", 1), move(far_down, "x", -1)
    up = jnp.concatenate([plus(above[:cut], up), above[cut:]])
    down = jnp.concatenate([below[:cut], plus(below[cut:], down)])
    up, down = move(up, "x", 1), move(down, "x", -1)
    return parts[0].astype(F32) + up.astype(F32) + down.astype(F32)


def gather_steps(block, axis, count, dim):
    half = block.shape[dim] // 2
    up = down = block
    for step in range(count // 2):
        if step == count // 2 - 1:
            up = lax.slice_in_dim(up, 0, half, axis=dim)
            down = lax.slice_in_dim(down, half, 2 * half, axis=dim)
        up, down = move(up, axis, 1), move(down, axis, -1)
        wait = yield up, down
        if wait:
            up, down = lax.optimization_barrier((up, down, *wait))[:2]


def in_order(block, arrivals):
    ups, downs = zip(*arrivals)
    return [block, *downs[:-1], ups[-1], downs[-1], *ups[-2::-1]]


def scatter_ring(parts, axis, last=()):
    count = len(parts)
    middle = count // 2
    half = parts[0].shape[-2] // 2

    def low(v):
        return v[..., :half, :]

    def high(v):
        return v[..., half:, :]

    up, down = move(low(parts[middle]), axis, 1), move(high(parts[middle]), axis, -1)
    above, below = parts[middle - 1], parts[middle + 1]
    up = jnp.concatenate([plus(low(above), up), high(above)], axis=-2)
    down = jnp.concatenate([low(below), plus(high(below), down)], axis=-2)
    for d in range(middle - 1, 0, -1):
        if d == 1 and last:
            up, down = after(up, *last), after(down, *last)
        up, down = move(up, axis, 1), move(down, axis, -1)
        if d > 1:
            up, down = plus(up, parts[d - 1]), plus(down, parts[count - d + 1])
    return parts[0].astype(F32) + up.astype(F32) + down.astype(F32)


PIECES = [[(z, x) for z in range(Z)] for x in range(X // 2)]
PIECES += [[(z, X // 2) for z in range(Z // 2)], [(z, X // 2) for z in range(Z // 2, Z)]]
PIECES += [[(z, x) for z in range(Z)] for x in range(X // 2 + 1, X)]


FAR = [(0, 1), (1, 3), (3, 6), (6, 8)]
RESULTS = 4 + len(FAR)


def attention_kernel(mine, slots, key_homes, value_homes, place, q_ref, g_ref, *refs):
    if mine == RING:
        *pieces, pairs, dk, work, sems = refs
        pieces, results = pieces[:-RESULTS], pieces[-RESULTS:]
    else:
        total_ref, table_ref, *results, pairs, dk, work, taps, sems = refs
        results = results[RESULTS:]
    o_ref, dq_ref, dk_ref, dv_ref, *far_refs = results
    pair = pl.program_id(0)

    def gathered(which, p, group):
        lanes = pl.ds(pl.multiple_of(place[2] * LANES, LANES), LANES)
        return pltpu.make_async_copy(
            table_ref.at[:, group, :, lanes],
            pairs.at[p, :, :, pl.ds(which * LANES, LANES)],
            sems.at[p, which],
        )

    def passed(which, p, group):
        jobs = []
        for piece, places in zip(pieces, PIECES):
            for i, (dz, dx) in enumerate(places):
                chip = lax.rem(place[0] + dz, Z) * X + lax.rem(place[1] + dx, X)
                jobs.append(
                    pltpu.make_async_copy(
                        piece.at[i, group],
                        pairs.at[p, pl.ds(chip * CORES, CORES), :, pl.ds(which * LANES, LANES)],
                        sems.at[p, which],
                    )
                )
        return jobs

    def copies(p):
        jobs = [gathered(w, p, i) for i, (w, q) in enumerate(GATHERED) if q == mine[p]]
        for i, (w, q) in enumerate(PASSED):
            if q == mine[p]:
                jobs += passed(w, p, i)
        return jobs

    @pl.when(pair == 0)
    def _():
        for p in range(len(mine)):
            for job in copies(p):
                job.start()

    dk[...] = jnp.zeros_like(dk)
    dv_ref[...] = jnp.zeros_like(dv_ref)

    for p in range(len(mine)):

        @pl.when(pair == p)
        def _(p=p):
            for job in copies(p):
                job.wait()

    left = lax.broadcasted_iota(jnp.int32, (BLOCK, LANES), 1) < HEAD_DIM
    none = jnp.zeros((LANES, LANES), BF16)

    def spread(v):
        zero = jnp.zeros_like(v)
        return jnp.concatenate([jnp.where(left, v, zero), jnp.where(left, zero, v)], axis=0)

    def merge(v):
        return jnp.where(left, v[:BLOCK], v[BLOCK:])

    def dot(a, b, dims):
        return lax.dot_general(a, b, dims, preferred_element_type=F32)

    def add(ref, home, part):
        at = (home // 4, pl.ds(pl.multiple_of(home % 4 * BLOCK, BLOCK), BLOCK), slice(None))
        ref[at] = (ref[at].astype(F32) + part).astype(BF16)

    scale = 1.0 / math.sqrt(HEAD_DIM)

    def visit(b):
        rows = slice(b * BLOCK, (b + 1) * BLOCK)
        both = jnp.concatenate(
            [
                pairs[
                    pair,
                    slots[b, j] // 2,
                    pl.ds(pl.multiple_of(slots[b, j] % 2 * BLOCK, BLOCK), BLOCK),
                    :,
                ]
                for j in range(SEL)
            ],
            axis=0,
        )
        query = spread((q_ref[rows, :].astype(F32) * scale).astype(BF16))
        grad = spread(g_ref[rows, :])
        sides = jnp.concatenate(
            [jnp.concatenate([query, none], axis=1), jnp.concatenate([none, grad], axis=1)], axis=0
        )
        chunks = [slice(c, c + CHUNK) for c in range(0, SEL * BLOCK, CHUNK)]
        keys_here, values_here = slice(0, LANES), slice(LANES, 2 * LANES)
        room = work.at[b % 2]
        top = None
        for c in chunks:
            products = dot(both[c], sides, (((1,), (1,)), ((), ())))
            room[c, :] = products
            highest = jnp.max(products[:, keys_here], axis=0, keepdims=True)
            top = highest if top is None else jnp.maximum(top, highest)
        mass = moment = 0.0
        for c in chunks:
            scores = jnp.exp(room[c, keys_here] - top)
            room[c, keys_here] = scores
            mass = mass + jnp.sum(scores, axis=0, keepdims=True)
            moment = moment + jnp.sum(scores * room[c, values_here], axis=0, keepdims=True)
        inverse = 1.0 / mass
        delta = moment * inverse
        sums = 0.0
        for c in chunks:
            probs = room[c, keys_here] * inverse
            slope = probs * (room[c, values_here] - delta)
            factors = jnp.concatenate([slope.astype(BF16), probs.astype(BF16)], axis=1)
            sums = sums + dot(factors, both[c], (((0,), (0,)), ((), ())))
            parts = dot(factors, sides, (((1,), (0,)), ((), ())))
            for i in range(CHUNK // BLOCK):
                part = slice(i * BLOCK, (i + 1) * BLOCK)
                j = c.start // BLOCK + i
                add(dk, key_homes[b, j], parts[part, :LANES])
                add(dv_ref, value_homes[b, j], parts[part, LANES:])
        dq_ref[rows, :] = (merge(sums[:LANES, :LANES]) * scale).astype(BF16)
        o_ref[rows, :] = merge(sums[LANES:, LANES:]).astype(BF16)

    for b in range(4):
        visit(b)

    for i in range(CHIPS):
        dk_ref[i] = dk[i, :KEPT, :]
        z, x = lax.rem(i % Z + FIRST + place[0], Z), i // Z
        dv_ref[i, ROWS + EXTRA :, :] = dk[z * X + x, KEPT:, :]

    if mine != RING:
        @pl.when(pair == 0)
        def _():
            for c in range(CHANNELS // LANES):
                part = slice(c * LANES, (c + 1) * LANES)
                taps[part] = total_ref[:, part].T
            odd = place[2] == 1
            blank = jnp.zeros((EXTRA, LANES - TAPS), F32)
            fill = jnp.zeros((EXTRA - WIDTH, TAPS), F32)

            def extra(i, carry):
                z, x = lax.rem(i % Z + FIRST + place[0], Z), lax.rem(i // Z + place[1], X)
                chip = z * X + x
                both = taps[pl.ds(pl.multiple_of(chip * 2 * WIDTH, 2 * WIDTH), 2 * WIDTH)]
                mine = jnp.where(odd, both[WIDTH:], both[:WIDTH])
                mine = jnp.concatenate([jnp.concatenate([mine, fill], axis=0), blank], axis=1)
                dv_ref[i, pl.ds(ROWS, EXTRA), :] = mine.astype(BF16)
                return carry

            lax.fori_loop(0, CHIPS, extra, 0)

    for ref, (first, end) in zip(far_refs, FAR):
        for i in range(first, end):
            ref[i - first] = dv_ref[X // 2 * Z + i]


def attention(slots, place, queries, grads, total, table, pieces):
    owner = slots // 2
    z, x = owner // (CORES * X), owner // CORES % X
    dz, dx = (z - place[0]) % Z, (x - place[1]) % X
    inner = owner % CORES * 2 + slots % 2
    key_homes = (z * X + dx) * 4 + inner
    value_homes = (dx * Z + (dz + Z - FIRST) % Z) * 4 + inner
    scalars = (slots, key_homes, value_homes, place)
    any_space = pl.BlockSpec(memory_space=pl.ANY)

    def call(mine, more, specs, held, scratch):
        lane_block = lambda rows: pl.BlockSpec((rows, LANES), lambda p, *_: (0, p + mine[0]))
        chip_block = lambda chips, rows: pl.BlockSpec(
            (chips, rows, LANES), lambda p, *_: (0, 0, p + mine[0])
        )
        shapes = [(ROWS,), (ROWS,), (CHIPS, KEPT), (CHIPS, SENT)]
        shapes += [(end - first, SENT) for first, end in FAR]
        inputs = (*scalars, queries, grads, *more)
        return pl.pallas_call(
            functools.partial(attention_kernel, mine),
            grid_spec=pltpu.PrefetchScalarGridSpec(
                num_scalar_prefetch=len(scalars),
                grid=(len(mine),),
                in_specs=[lane_block(ROWS), lane_block(ROWS), *specs, *[any_space] * len(held)],
                out_specs=[
                    lane_block(*shape) if len(shape) == 1 else chip_block(*shape) for shape in shapes
                ],
                scratch_shapes=[
                    pltpu.VMEM((len(mine), CHIPS * CORES, ROWS // CORES, 2 * LANES), BF16),
                    pltpu.VMEM((CHIPS, ROWS, LANES), BF16),
                    pltpu.VMEM((2, SEL * BLOCK, 2 * LANES), F32),
                    *scratch,
                    pltpu.SemaphoreType.DMA((len(mine), 2)),
                ],
            ),
            out_shape=[jax.ShapeDtypeStruct((*shape, HALF_INNER), BF16) for shape in shapes],
            input_output_aliases={len(inputs) + i: i for i in range(len(held))},
            compiler_params=pltpu.CompilerParams(
                dimension_semantics=("arbitrary",), vmem_limit_bytes=50 * 1024 * 1024
            ),
            cost_estimate=pl.CostEstimate(
                flops=1_600_000_000 * len(mine),
                bytes_accessed=9_000_000 * len(mine),
                transcendentals=530_000 * len(mine),
            ),
            name="attend",
        )(*inputs, *held)

    held = call(RING, pieces, [any_space] * len(pieces), (), ())
    whole = pl.BlockSpec((TAPS, CHANNELS), lambda p, *_: (0, 0))
    return call(
        TABLE, (total, table), [whole, any_space], held, [pltpu.VMEM((CHANNELS, TAPS), F32)]
    )


def conv_kernel(x_ref, g_ref, before_ref, after_ref, w_ref, out_ref, dx_ref, dw_ref, xs, hs):
    frames = x_ref.shape[0]
    xs[0:32] = before_ref[0:32].astype(F32)
    xs[32 : 32 + frames] = x_ref[...].astype(F32)
    xs[32 + frames : 64 + frames] = after_ref[0:32].astype(F32)
    wide = frames + 32
    pre = jnp.zeros((wide, LANES), F32)
    for j in range(KERNEL):
        pre = pre + w_ref[j : j + 1, :] * xs[j + 1 : j + 1 + wide]
    gate = 1.0 / (1.0 + jnp.exp(-pre))
    out_ref[...] = (pre * gate)[16 : 16 + frames].astype(BF16)
    incoming = jnp.concatenate(
        [before_ref[32:48], g_ref[...], after_ref[32:48]], axis=0
    ).astype(F32)
    hidden = (incoming * gate * (1.0 + pre * (1.0 - gate))).astype(BF16).astype(F32)
    hs[...] = hidden
    total = jnp.zeros((frames, LANES), F32)
    for j in range(KERNEL):
        total = total + w_ref[j : j + 1, :] * hs[31 - j : 31 - j + frames]
    dx_ref[...] = total.astype(BF16)
    centre = hidden[16 : 16 + frames]
    for j in range(KERNEL):
        product = xs[j + 17 : j + 17 + frames] * centre
        dw_ref[j : j + 1, :] = jnp.sum(product, axis=0, keepdims=True)
    dw_ref[KERNEL:, :] = jnp.zeros((1, LANES), F32)


def convolve(x, g, before, after, weight):
    frames, channels = x.shape
    block = lambda rows: pl.BlockSpec((rows, LANES), lambda p: (0, p))
    return pl.pallas_call(
        conv_kernel,
        grid=(channels // LANES,),
        in_specs=[block(frames), block(frames), block(48), block(48), block(KERNEL)],
        out_specs=[block(frames), block(frames), block(KERNEL + 1)],
        out_shape=[
            jax.ShapeDtypeStruct((frames, channels), BF16),
            jax.ShapeDtypeStruct((frames, channels), BF16),
            jax.ShapeDtypeStruct((KERNEL + 1, channels), F32),
        ],
        scratch_shapes=[pltpu.VMEM((frames + 64, LANES), F32), pltpu.VMEM((frames + 32, LANES), F32)],
        compiler_params=pltpu.CompilerParams(dimension_semantics=("arbitrary",)),
        cost_estimate=pl.CostEstimate(
            flops=20_000_000, bytes_accessed=1_000_000, transcendentals=120_000
        ),
        name="conv",
    )(x, g, before, after, weight)


def body(queries, keys, values, out_grad, picks, conv_in, conv_weight, conv_grad):
    me = lax.axis_index("ctx")
    core = me % CORES
    my_x = (me // CORES) % X
    my_z = me // (CORES * X)
    frames = queries.shape[1]

    def lanes(which, p, side):
        start = side * HALF_INNER + p * LANES
        return (keys, values)[which][0, :, start : start + LANES]

    table = lax.all_gather(
        jnp.stack([jnp.concatenate([lanes(w, p, 0), lanes(w, p, 1)], axis=1) for w, p in GATHERED]),
        "ctx",
    )
    flip = core == 1
    sides = [jnp.stack([lanes(w, p, side) for w, p in PASSED]) for side in range(CORES)]
    mine = jnp.where(flip, sides[1], sides[0])
    taken = swap_cores(jnp.where(flip, sides[0], sides[1]))
    block = jnp.stack([jnp.where(flip, taken, mine), jnp.where(flip, mine, taken)], axis=1)
    steps = gather_steps(block[None], "z", Z, 2)
    column = [next(steps)]
    for _ in range(Z // 2 - 1):
        column.append(steps.send(None))
    column = in_order(block[None], column)
    middle = Z // 2
    column[middle : middle + 2] = [jnp.concatenate(column[middle : middle + 2], axis=2)]
    column = jnp.concatenate(column)
    steps = gather_steps(column, "x", X, 0)
    pieces = [next(steps)]
    for _ in range(X // 2 - 1):
        pieces.append(steps.send(None))
    pieces = in_order(column, pieces)

    packed = jnp.stack([queries[0], out_grad[0]])
    first, second = packed[:, :, :HALF_INNER], packed[:, :, HALF_INNER:]
    taken = swap_cores(jnp.where(flip, first, second))
    chip = jnp.concatenate([jnp.where(flip, second, first), taken], axis=1)
    slots = jnp.concatenate([picks[0], swap_cores(picks[0])], axis=0)

    ends = CHIPS * CORES - 1
    tail = jnp.concatenate([conv_in[0, frames - 32 :], conv_grad[0, frames - 16 :]], axis=0)
    head = jnp.concatenate([conv_in[0, :32], conv_grad[0, :16]], axis=0)
    before = lax.ppermute(tail, "ctx", [(i, i + 1) for i in range(ends)])
    behind = lax.ppermute(head, "ctx", [(i + 1, i) for i in range(ends)])
    conv_out, conv_dx, partial = convolve(conv_in[0], conv_grad[0], before, behind, conv_weight)

    total = partial + swap_cores(partial)
    total = total + lax.ppermute(total, "dp", [(i, i ^ 1) for i in range(4)])
    total = total + lax.ppermute(total, "dp", [(i, i ^ 2) for i in range(4)])

    attended, query_grad, key_parts, value_parts, *far_parts = attention(
        slots, jnp.stack([my_z, my_x, core]), chip[0], chip[1], total, table, pieces
    )

    key_parts = key_parts.reshape(Z, X, KEPT, HALF_INNER)
    value_parts = value_parts.reshape(X, Z, SENT, HALF_INNER)
    key_sum = lax.psum_scatter(
        key_parts, "ctx", scatter_dimension=0, axis_index_groups=COLUMNS
    )
    key_near = [move(key_sum[1], "x", 1), move(key_sum[2], "x", 2), move(key_sum[3], "x", -1)]
    early = scatter_across([value_parts[d, :FIRST] for d in range(X)], *far_parts[:2]).astype(BF16)
    late = scatter_across([value_parts[d, FIRST:] for d in range(X)], *far_parts[2:]).astype(BF16)
    by_z = [early[d] for d in range(FIRST)] + [late[d] for d in range(Z - FIRST)]
    value_sum = scatter_ring([by_z[(d + Z - FIRST) % Z] for d in range(Z)], "z", (key_sum,))
    key_sum = key_sum[0].astype(F32) + sum(near.astype(F32) for near in key_near)
    key_total = jnp.concatenate([key_sum, value_sum[ROWS + EXTRA :]]).astype(BF16)
    value_total = value_sum[:ROWS].astype(BF16)
    weight_grad = value_sum[ROWS : ROWS + WIDTH, :KERNEL].T / math.sqrt(
        conv_in.shape[0] * lax.axis_size("dp") * frames * CHIPS * CORES
    )

    def whole(own, siblings):
        other = swap_cores(siblings)
        return jnp.concatenate([jnp.where(flip, other, own), jnp.where(flip, own, other)], axis=2)

    early = jnp.stack([attended, query_grad])
    early = whole(early[:, :frames], early[:, frames:])
    late = jnp.stack([key_total, value_total])
    lower, upper = late[:, :frames], late[:, frames:]
    late = whole(jnp.where(flip, upper, lower), jnp.where(flip, lower, upper))
    return (
        early[0][None],
        early[1][None],
        late[0][None],
        late[1][None],
        conv_out[None],
        conv_dx[None],
        weight_grad,
    )


def solution(mesh):
    rows = P("dp", "ctx", None)
    return jax.shard_map(
        body,
        mesh=mesh,
        in_specs=(rows, rows, rows, rows, rows, rows, P(), rows),
        out_specs=(rows, rows, rows, rows, rows, rows, P(None, "ctx")),
        check_vma=False,
    )
```

profile of v0, /device:TPU:25, one launch (start us, length us, event | category | flops | bytes accessed | tf_op | source)
XLA Modules:
  0.0 252.5 jit_solution(18045448192201235113)
XLA Ops:
  13.3 4.0 %collective-permute-start.8 = (bf16[1,2,2,128,128]{4,3,2,1,0:T(8,128)(2,1)S(1)}, bf16[1,2,2,128,128]{4,3,2,1,0:T(8,128)(2,1)S(1)}, u32[]{:S(2)}, u32[]{:S(2)}) collective-permute-start(bf16[1,2,2,128,128]{4,3,2,1,0:T(8,128)(2,1)S(1)} %maximum_bitcast_fusion), channel_id=1, source_target_pairs={{0,56},{1,57},{2,58},{3,59},{4,60},{5,61},{6,62},{7,63},{8,0},{9,1... | collective-permute-start | bytes 393224 | tf_op jit(solution)/shard_map/ppermute | solution.py:50
  17.3 3.5 %collective-permute-done.11 = bf16[1,2,2,128,128]{4,3,2,1,0:T(8,128)(2,1)S(1)} collective-permute-done((bf16[1,2,2,128,128]{4,3,2,1,0:T(8,128)(2,1)S(1)}, bf16[1,2,2,128,128]{4,3,2,1,0:T(8,128)(2,1)S(1)}, u32[]{:S(2)}, u32[]{:S(2)}) %collective-permute-start.11) | collective-permute-done | bytes 131104 | tf_op jit(solution)/shard_map/ppermute | solution.py:50
  30.2 2.8 %collective-permute-done.13 = bf16[1,2,2,128,128]{4,3,2,1,0:T(8,128)(2,1)S(1)} collective-permute-done((bf16[1,2,2,128,128]{4,3,2,1,0:T(8,128)(2,1)S(1)}, bf16[1,2,2,128,128]{4,3,2,1,0:T(8,128)(2,1)S(1)}, u32[]{:S(2)}, u32[]{:S(2)}) %collective-permute-start.13) | collective-permute-done | bytes 131104 | tf_op jit(solution)/shard_map/ppermute | solution.py:50
  33.0 2.7 %collective-permute-start.15 = (bf16[1,2,1,128,128]{4,3,2,1,0:T(8,128)(2,1)S(1)}, bf16[1,2,1,128,128]{4,3,2,1,0:T(8,128)(2,1)S(1)}, u32[]{:S(2)}, u32[]{:S(2)}) collective-permute-start(bf16[1,2,1,128,128]{4,3,2,1,0:T(8,128)(2,1)S(1)} %slice.310), channel_id=1, source_target_pairs={{0,56},{1,57},{2,58},{3,59},{4,60},{5,61},{6,62},{7,63},{8,0},{9,1... | collective-permute-start | bytes 196616 | tf_op jit(solution)/shard_map/ppermute | solution.py:50
  44.1 5.4 %collective-permute-start.2 = (bf16[48,768]{1,0:T(8,128)(2,1)S(1)}, bf16[48,768]{1,0:T(8,128)(2,1)S(1)}, u32[]{:S(2)}, u32[]{:S(2)}) collective-permute-start(bf16[48,768]{1,0:T(8,128)(2,1)S(1)} %pad_maximum_fusion.12), channel_id=1, source_target_pairs={{0,1},{1,2},{2,3},{3,4},{4,5},{5,6},{6,7},{7,8},{8,9},{9,10},{10,1... | collective-permute-start | bytes 221192 | tf_op jit(solution)/shard_map/ppermute | solution.py:435
  51.6 12.7 %collective-permute-done.17.refs_4_ = bf16[8,2,2,128,128]{4,3,2,1,0:T(8,128)(2,1)S(1)} collective-permute-done((bf16[8,2,2,128,128]{4,3,2,1,0:T(8,128)(2,1)}, bf16[8,2,2,128,128]{4,3,2,1,0:T(8,128)(2,1)S(1)}, u32[]{:S(2)}, u32[]{:S(2)}) %collective-permute-start.17) | collective-permute-done | bytes 1048608 | tf_op jit(solution)/shard_map/ppermute | solution.py:50
  69.4 9.5 %collective-permute-start.1 = (bf16[2,128,384]{2,1,0:T(8,128)(2,1)S(1)}, bf16[2,128,384]{2,1,0:T(8,128)(2,1)S(1)}, u32[]{:S(2)}, u32[]{:S(2)}) collective-permute-start(bf16[2,128,384]{2,1,0:T(8,128)(2,1)S(1)} %get-tuple-element.82), channel_id=1, source_target_pairs={{0,1},{1,0},{2,3},{3,2},{4,5},{5,4},{6,7},{7,6},{8,9},{9,8},{10,11... | collective-permute-start | bytes 589832 | tf_op jit(solution)/shard_map/ppermute | solution.py:61
  79.6 5.2 %conv.1 = (bf16[128,768]{1,0:T(8,128)(2,1)}, bf16[128,768]{1,0:T(8,128)(2,1)}, f32[32,768]{1,0:T(8,128)}) custom-call(bf16[128,768]{1,0:T(8,128)(2,1)} %bitcast.174, bf16[128,768]{1,0:T(8,128)(2,1)} %bitcast.175, bf16[48,768]{1,0:T(8,128)(2,1)} %copy-done.6, bf16[48,768]{1,0:T(8,128)(2,1)} %copy-done.7, f32[31,768]{1,0:T(8,128)} %w_ref.1), custom_call_target="tpu_custom_call" | custom-call | flops 20000000 | bytes 1000000 | tf_op jit(solution)/shard_map/conv/pallas_call | solution.py:373
  87.4 4.2 %collective-permute-done.5 = f32[32,768]{1,0:T(8,128)S(1)} collective-permute-done((f32[32,768]{1,0:T(8,128)S(1)}, f32[32,768]{1,0:T(8,128)S(1)}, u32[]{:S(2)}, u32[]{:S(2)}) %collective-permute-start.5) | collective-permute-done | bytes 98336 | tf_op jit(solution)/shard_map/ppermute | solution.py:440
  92.6 4.1 %collective-permute-done.6 = f32[32,768]{1,0:T(8,128)S(1)} collective-permute-done((f32[32,768]{1,0:T(8,128)S(1)}, f32[32,768]{1,0:T(8,128)S(1)}, u32[]{:S(2)}, u32[]{:S(2)}) %collective-permute-start.6) | collective-permute-done | bytes 98336 | tf_op jit(solution)/shard_map/ppermute | solution.py:441
  98.6 8.5 %attend.2 = (bf16[256,384]{1,0:T(8,128)(2,1)S(1)}, bf16[256,384]{1,0:T(8,128)(2,1)S(1)}, bf16[32,224,384]{2,1,0:T(8,128)(2,1)}, bf16[32,304,384]{2,1,0:T(8,128)(...) custom-call(s32[4,16]{1,0:T(4,128)S(1)} %get-tuple-element.103.slots, ...), custom_call_target="tpu_custom_call" | custom-call | flops 1600000000 | bytes 9000000 | tf_op jit(solution)/shard_map/attend/pallas_call | solution.py:306
  107.1 18.9 %all-gather.3.cloned.1.call-done = bf16[256,128,256]{2,1,0:T(8,128)(2,1)} async-done(((bf16[4,128,256]{2,1,0:T(8,128)(2,1)}), bf16[256,128,256]{2,1,0:T(8,128)(2,1)}) %all-gather.3.cloned.1.call-update) | async-done | bytes 16777232 | tf_op jit(solution)/shard_map/all_gather | solution.py:403
  126.0 13.6 %attend.3 = (bf16[256,384]{1,0:T(8,128)(2,1)S(1)}, bf16[256,384]{1,0:T(8,128)(2,1)S(1)}, bf16[32,224,384]{2,1,0:T(8,128)(2,1)}, bf16[32,304,384]{2,1,0:T(8,128)(...) custom-call(s32[4,16]{1,0:T(4,128)S(1)} %get-tuple-element.103.slots, ...), custom_call_target="tpu_custom_call", output_to_operand_aliasing={{0}: (8, {}), {1}: (9, {}), {2}: (10, {}), {3}: (11, {}), {... | custom-call | flops 3200000000 | bytes 18000000 | tf_op jit(solution)/shard_map/attend/pallas_call | solution.py:306
  140.8 10.3 %collective-permute-start.26 = (bf16[2,304,384]{2,1,0:T(8,128)(2,1)S(1)}, bf16[2,304,384]{2,1,0:T(8,128)(2,1)S(1)}, u32[]{:S(2)}, u32[]{:S(2)}) collective-permute-start(bf16[2,304,384]{2,1,0:T(8,128)(2,1)S(1)} %get-tuple-element.42), channel_id=1, source_target_pairs={{0,6},{1,7},{2,0},{3,1},{4,2},{5,3},{6,4},{7,5},{8,14},{9,15},{10,... | collective-permute-start | bytes 1400840 | tf_op jit(solution)/shard_map/ppermute | solution.py:50
  156.0 5.1 %collective-permute-done.26 = bf16[2,304,384]{2,1,0:T(8,128)(2,1)S(1)} collective-permute-done((bf16[2,304,384]{2,1,0:T(8,128)(2,1)S(1)}, bf16[2,304,384]{2,1,0:T(8,128)(2,1)S(1)}, u32[]{:S(2)}, u32[]{:S(2)}) %collective-permute-start.26) | collective-permute-done | bytes 466976 | tf_op jit(solution)/shard_map/ppermute | solution.py:50
  161.2 10.0 %collective-permute-done.30 = bf16[2,304,384]{2,1,0:T(8,128)(2,1)S(1)} collective-permute-done((bf16[2,304,384]{2,1,0:T(8,128)(2,1)S(1)}, bf16[2,304,384]{2,1,0:T(8,128)(2,1)S(1)}, u32[]{:S(2)}, u32[]{:S(2)}) %collective-permute-start.30) | collective-permute-done | bytes 466976 | tf_op jit(solution)/shard_map/ppermute | solution.py:50
  172.7 3.0 %collective-permute-start.31 = (bf16[3,304,384]{2,1,0:T(8,128)(2,1)S(1)}, bf16[3,304,384]{2,1,0:T(8,128)(2,1)S(1)}, u32[]{:S(2)}, u32[]{:S(2)}) collective-permute-start(bf16[3,304,384]{2,1,0:T(8,128)(2,1)S(1)} %pad_maximum_fusion.3), channel_id=1, source_target_pairs={{0,6},{1,7},{2,0},{3,1},{4,2},{5,3},{6,4},{7,5},{8,14},{9,15},{10,... | collective-permute-start | bytes 2101256 | tf_op jit(solution)/shard_map/ppermute | solution.py:50
  178.8 7.7 %collective-permute-done.29 = bf16[3,304,384]{2,1,0:T(8,128)(2,1)S(1)} collective-permute-done((bf16[3,304,384]{2,1,0:T(8,128)(2,1)S(1)}, bf16[3,304,384]{2,1,0:T(8,128)(2,1)S(1)}, u32[]{:S(2)}, u32[]{:S(2)}) %collective-permute-start.29) | collective-permute-done | bytes 700448 | tf_op jit(solution)/shard_map/ppermute | solution.py:50
  186.5 3.0 %collective-permute-done.31 = bf16[3,304,384]{2,1,0:T(8,128)(2,1)S(1)} collective-permute-done((bf16[3,304,384]{2,1,0:T(8,128)(2,1)S(1)}, bf16[3,304,384]{2,1,0:T(8,128)(2,1)S(1)}, u32[]{:S(2)}, u32[]{:S(2)}) %collective-permute-start.31) | collective-permute-done | bytes 700448 | tf_op jit(solution)/shard_map/ppermute | solution.py:50
  195.8 4.5 %collective-permute-done.32 = bf16[152,384]{1,0:T(8,128)(2,1)S(1)} collective-permute-done((bf16[152,384]{1,0:T(8,128)(2,1)S(1)}, bf16[152,384]{1,0:T(8,128)(2,1)S(1)}, u32[]{:S(2)}, u32[]{:S(2)}) %collective-permute-start.32) | collective-permute-done | bytes 116768 | tf_op jit(solution)/shard_map/ppermute | solution.py:50
  200.4 2.7 %collective-permute-start.37 = (bf16[304,384]{1,0:T(8,128)(2,1)S(1)}, bf16[304,384]{1,0:T(8,128)(2,1)S(1)}, u32[]{:S(2)}, u32[]{:S(2)}) collective-permute-start(bf16[304,384]{1,0:T(8,128)(2,1)S(1)} %pad_maximum_fusion.7), channel_id=1, source_target_pairs={{0,56},{1,57},{2,58},{3,59},{4,60},{5,61},{6,62},{7,63},{8,0},{9,1... | collective-permute-start | bytes 700424 | tf_op jit(solution)/shard_map/ppermute | solution.py:50
  203.3 11.2 %collective-permute-done.27 = bf16[5,304,384]{2,1,0:T(8,128)(2,1)S(1)} collective-permute-done((bf16[5,304,384]{2,1,0:T(8,128)(2,1)S(1)}, bf16[5,304,384]{2,1,0:T(8,128)(2,1)S(1)}, u32[]{:S(2)}, u32[]{:S(2)}) %collective-permute-start.27) | collective-permute-done | bytes 1167392 | tf_op jit(solution)/shard_map/ppermute | solution.py:50
  219.1 2.9 %collective-permute-start.38 = (bf16[304,384]{1,0:T(8,128)(2,1)S(1)}, bf16[304,384]{1,0:T(8,128)(2,1)S(1)}, u32[]{:S(2)}, u32[]{:S(2)}) collective-permute-start(bf16[304,384]{1,0:T(8,128)(2,1)S(1)} %get-tuple-element.62), channel_id=1, source_target_pairs={{0,56},{1,57},{2,58},{3,59},{4,60},{5,61},{6,62},{7,63},{8,0},{9,1... | collective-permute-start | bytes 700424 | tf_op jit(solution)/shard_map/ppermute | solution.py:50
  234.7 8.8 %collective-permute-start.40 = (bf16[2,128,384]{2,1,0:T(8,128)(2,1)S(1)}, bf16[2,128,384]{2,1,0:T(8,128)(2,1)S(1)}, u32[]{:S(2)}, u32[]{:S(2)}) collective-permute-start(bf16[2,128,384]{2,1,0:T(8,128)(2,1)S(1)} %broadcast_select_fusion.3), channel_id=1, source_target_pairs={{0,1},{1,0},{2,3},{3,2},{4,5},{5,4},{6,7},{7,6},{8,9},{9,8},{10,11... | collective-permute-start | bytes 589832 | tf_op jit(solution)/shard_map/ppermute | solution.py:61
  (149 shorter events, 73.2 us)
Async XLA Ops:
  7.2 118.9 %all-gather.3.cloned.1.call-start = ((), (), s32[]{:S(2)}) async-start(), calls=%async_computation.2 | async-start | bytes 17039360 | tf_op jit(solution)/shard_map/all_gather | solution.py:403
  9.8 212.2 %reduce-scatter.2.cloned.1.call-start = ((), (), s32[]{:S(2)}) async-start(), calls=%async_computation.1 | async-start | bytes 6193152 | tf_op jit(solution)/shard_map/reduce_scatter | solution.py:449
  11.6 9.2 %collective-permute-start.11 = (bf16[1,2,2,128,128]{4,3,2,1,0:T(8,128)(2,1)S(1)}, bf16[1,2,2,128,128]{4,3,2,1,0:T(8,128)(2,1)S(1)}, u32[]{:S(2)}, u32[]{:S(2)}) collective-permute-start(bf16[1,2,2,128,128]{4,3,2,1,0:T(8,128)(2,1)S(1)} %maximum_bitcast_fusion), channel_id=1, source_target_pairs={{0,8},{1,9},{2,10},{3,11},{4,12},{5,13},{6,14},{7,15},{8,16},{9,17... | collective-permute-start | bytes 393224 | tf_op jit(solution)/shard_map/ppermute | solution.py:50
  23.5 61.3 %collective-permute-start = (s32[2,16]{1,0:T(2,128)S(1)}, s32[2,16]{1,0:T(2,128)S(1)}, u32[]{:S(2)}, u32[]{:S(2)}) collective-permute-start(s32[2,16]{1,0:T(2,128)S(1)} %bitcast.176), channel_id=1, source_target_pairs={{0,1},{1,0},{2,3},{3,2},{4,5},{5,4},{6,7},{7,6},{8,9},{9,8},{10,11... | collective-permute-start | bytes 392 | tf_op jit(solution)/shard_map/ppermute | solution.py:61
  40.3 24.1 %collective-permute-start.17 = (bf16[8,2,2,128,128]{4,3,2,1,0:T(8,128)(2,1)}, bf16[8,2,2,128,128]{4,3,2,1,0:T(8,128)(2,1)S(1)}, u32[]{:S(2)}, u32[]{:S(2)}) collective-permute-start(bf16[8,2,2,128,128]{4,3,2,1,0:T(8,128)(2,1)} %constant_dynamic-update-slice_fusion.2.refs_0_), channel_id=1, source_target_pairs={{0,2},{1,3},{2,4},{3,5},{4,6},{5,7},{6,0},{7,1},{8,10},{9,11},{10,... | collective-permute-start | bytes 3145736 | tf_op jit(solution)/shard_map/ppermute | solution.py:50
  41.8 23.7 %collective-permute-start.16 = (bf16[8,2,2,128,128]{4,3,2,1,0:T(8,128)(2,1)}, bf16[8,2,2,128,128]{4,3,2,1,0:T(8,128)(2,1)}, u32[]{:S(2)}, u32[]{:S(2)}) collective-permute-start(bf16[8,2,2,128,128]{4,3,2,1,0:T(8,128)(2,1)} %constant_dynamic-update-slice_fusion.2.refs_0_), channel_id=1, source_target_pairs={{0,6},{1,7},{2,0},{3,1},{4,2},{5,3},{6,4},{7,5},{8,14},{9,15},{10,... | collective-permute-start | bytes 3145736 | tf_op jit(solution)/shard_map/ppermute | solution.py:50
  44.1 25.3 %collective-permute-start.2 = (bf16[48,768]{1,0:T(8,128)(2,1)S(1)}, bf16[48,768]{1,0:T(8,128)(2,1)S(1)}, u32[]{:S(2)}, u32[]{:S(2)}) collective-permute-start(bf16[48,768]{1,0:T(8,128)(2,1)S(1)} %pad_maximum_fusion.12), channel_id=1, source_target_pairs={{0,1},{1,2},{2,3},{3,4},{4,5},{5,6},{6,7},{7,8},{8,9},{9,10},{10,1... | collective-permute-start | bytes 221192 | tf_op jit(solution)/shard_map/ppermute | solution.py:435
  49.6 29.4 %collective-permute-start.3 = (bf16[48,768]{1,0:T(8,128)(2,1)S(1)}, bf16[48,768]{1,0:T(8,128)(2,1)S(1)}, u32[]{:S(2)}, u32[]{:S(2)}) collective-permute-start(bf16[48,768]{1,0:T(8,128)(2,1)S(1)} %pad_maximum_fusion.13), channel_id=1, source_target_pairs={{1,0},{2,1},{3,2},{4,3},{5,4},{6,5},{7,6},{8,7},{9,8},{10,9},{11,1... | collective-permute-start | bytes 221192 | tf_op jit(solution)/shard_map/ppermute | solution.py:436
  65.4 31.3 %collective-permute-start.18 = (bf16[4,2,2,128,128]{4,3,2,1,0:T(8,128)(2,1)S(1)}, bf16[4,2,2,128,128]{4,3,2,1,0:T(8,128)(2,1)S(1)}, u32[]{:S(2)}, u32[]{:S(2)}) collective-permute-start(bf16[4,2,2,128,128]{4,3,2,1,0:T(8,128)(2,1)S(1)} %slice.311), channel_id=1, source_target_pairs={{0,2},{1,3},{2,4},{3,5},{4,6},{5,7},{6,0},{7,1},{8,10},{9,11},{10,... | collective-permute-start | bytes 1572872 | tf_op jit(solution)/shard_map/ppermute | solution.py:50
  66.6 30.1 %collective-permute-start.19 = (bf16[4,2,2,128,128]{4,3,2,1,0:T(8,128)(2,1)S(1)}, bf16[4,2,2,128,128]{4,3,2,1,0:T(8,128)(2,1)S(1)}, u32[]{:S(2)}, u32[]{:S(2)}) collective-permute-start(bf16[4,2,2,128,128]{4,3,2,1,0:T(8,128)(2,1)S(1)} %slice.312), channel_id=1, source_target_pairs={{0,6},{1,7},{2,0},{3,1},{4,2},{5,3},{6,4},{7,5},{8,14},{9,15},{10,... | collective-permute-start | bytes 1572872 | tf_op jit(solution)/shard_map/ppermute | solution.py:50
  69.4 23.2 %collective-permute-start.1 = (bf16[2,128,384]{2,1,0:T(8,128)(2,1)S(1)}, bf16[2,128,384]{2,1,0:T(8,128)(2,1)S(1)}, u32[]{:S(2)}, u32[]{:S(2)}) collective-permute-start(bf16[2,128,384]{2,1,0:T(8,128)(2,1)S(1)} %get-tuple-element.82), channel_id=1, source_target_pairs={{0,1},{1,0},{2,3},{3,2},{4,5},{5,4},{6,7},{7,6},{8,9},{9,8},{10,11... | collective-permute-start | bytes 589832 | tf_op jit(solution)/shard_map/ppermute | solution.py:61
  139.7 15.1 %collective-permute-start.28 = (bf16[1,304,384]{2,1,0:T(8,128)(2,1)S(1)}, bf16[1,304,384]{2,1,0:T(8,128)(2,1)S(1)}, u32[]{:S(2)}, u32[]{:S(2)}) collective-permute-start(bf16[1,304,384]{2,1,0:T(8,128)(2,1)S(1)} %get-tuple-element.43), channel_id=1, source_target_pairs={{0,2},{1,3},{2,4},{3,5},{4,6},{5,7},{6,0},{7,1},{8,10},{9,11},{10,... | collective-permute-start | bytes 700424 | tf_op jit(solution)/shard_map/ppermute | solution.py:50
  140.8 20.4 %collective-permute-start.26 = (bf16[2,304,384]{2,1,0:T(8,128)(2,1)S(1)}, bf16[2,304,384]{2,1,0:T(8,128)(2,1)S(1)}, u32[]{:S(2)}, u32[]{:S(2)}) collective-permute-start(bf16[2,304,384]{2,1,0:T(8,128)(2,1)S(1)} %get-tuple-element.42), channel_id=1, source_target_pairs={{0,6},{1,7},{2,0},{3,1},{4,2},{5,3},{6,4},{7,5},{8,14},{9,15},{10,... | collective-permute-start | bytes 1400840 | tf_op jit(solution)/shard_map/ppermute | solution.py:50
  151.1 20.1 %collective-permute-start.30 = (bf16[2,304,384]{2,1,0:T(8,128)(2,1)S(1)}, bf16[2,304,384]{2,1,0:T(8,128)(2,1)S(1)}, u32[]{:S(2)}, u32[]{:S(2)}) collective-permute-start(bf16[2,304,384]{2,1,0:T(8,128)(2,1)S(1)} %get-tuple-element.44), channel_id=1, source_target_pairs={{0,6},{1,7},{2,0},{3,1},{4,2},{5,3},{6,4},{7,5},{8,14},{9,15},{10,... | collective-permute-start | bytes 1400840 | tf_op jit(solution)/shard_map/ppermute | solution.py:50
  154.0 24.9 %collective-permute-start.24 = (bf16[3,304,384]{2,1,0:T(8,128)(2,1)S(1)}, bf16[3,304,384]{2,1,0:T(8,128)(2,1)S(1)}, u32[]{:S(2)}, u32[]{:S(2)}) collective-permute-start(bf16[3,304,384]{2,1,0:T(8,128)(2,1)S(1)} %get-tuple-element.41), channel_id=1, source_target_pairs={{0,2},{1,3},{2,4},{3,5},{4,6},{5,7},{6,0},{7,1},{8,10},{9,11},{10,... | collective-permute-start | bytes 2101256 | tf_op jit(solution)/shard_map/ppermute | solution.py:50
  155.9 30.5 %collective-permute-start.29 = (bf16[3,304,384]{2,1,0:T(8,128)(2,1)S(1)}, bf16[3,304,384]{2,1,0:T(8,128)(2,1)S(1)}, u32[]{:S(2)}, u32[]{:S(2)}) collective-permute-start(bf16[3,304,384]{2,1,0:T(8,128)(2,1)S(1)} %pad_maximum_fusion.2), channel_id=1, source_target_pairs={{0,2},{1,3},{2,4},{3,5},{4,6},{5,7},{6,0},{7,1},{8,10},{9,11},{10,... | collective-permute-start | bytes 2101256 | tf_op jit(solution)/shard_map/ppermute | solution.py:50
  172.7 16.7 %collective-permute-start.31 = (bf16[3,304,384]{2,1,0:T(8,128)(2,1)S(1)}, bf16[3,304,384]{2,1,0:T(8,128)(2,1)S(1)}, u32[]{:S(2)}, u32[]{:S(2)}) collective-permute-start(bf16[3,304,384]{2,1,0:T(8,128)(2,1)S(1)} %pad_maximum_fusion.3), channel_id=1, source_target_pairs={{0,6},{1,7},{2,0},{3,1},{4,2},{5,3},{6,4},{7,5},{8,14},{9,15},{10,... | collective-permute-start | bytes 2101256 | tf_op jit(solution)/shard_map/ppermute | solution.py:50
  175.8 16.4 %collective-permute-start.20 = (bf16[2,128,384]{2,1,0:T(8,128)(2,1)S(1)}, bf16[2,128,384]{2,1,0:T(8,128)(2,1)S(1)}, u32[]{:S(2)}, u32[]{:S(2)}) collective-permute-start(bf16[2,128,384]{2,1,0:T(8,128)(2,1)S(1)} %fusion.18), channel_id=1, source_target_pairs={{0,1},{1,0},{2,3},{3,2},{4,5},{5,4},{6,7},{7,6},{8,9},{9,8},{10,11... | collective-permute-start | bytes 589832 | tf_op jit(solution)/shard_map/ppermute | solution.py:61
  178.7 35.7 %collective-permute-start.27 = (bf16[5,304,384]{2,1,0:T(8,128)(2,1)S(1)}, bf16[5,304,384]{2,1,0:T(8,128)(2,1)S(1)}, u32[]{:S(2)}, u32[]{:S(2)}) collective-permute-start(bf16[5,304,384]{2,1,0:T(8,128)(2,1)S(1)} %pad_maximum_fusion.1), channel_id=1, source_target_pairs={{0,6},{1,7},{2,0},{3,1},{4,2},{5,3},{6,4},{7,5},{8,14},{9,15},{10,... | collective-permute-start | bytes 3502088 | tf_op jit(solution)/shard_map/ppermute | solution.py:50
  191.4 25.7 %collective-permute-start.25 = (bf16[5,304,384]{2,1,0:T(8,128)(2,1)S(1)}, bf16[5,304,384]{2,1,0:T(8,128)(2,1)S(1)}, u32[]{:S(2)}, u32[]{:S(2)}) collective-permute-start(bf16[5,304,384]{2,1,0:T(8,128)(2,1)S(1)} %pad_maximum_fusion), channel_id=1, source_target_pairs={{0,2},{1,3},{2,4},{3,5},{4,6},{5,7},{6,0},{7,1},{8,10},{9,11},{10,... | collective-permute-start | bytes 3502088 | tf_op jit(solution)/shard_map/ppermute | solution.py:50
  192.3 8.0 %collective-permute-start.32 = (bf16[152,384]{1,0:T(8,128)(2,1)S(1)}, bf16[152,384]{1,0:T(8,128)(2,1)S(1)}, u32[]{:S(2)}, u32[]{:S(2)}) collective-permute-start(bf16[152,384]{1,0:T(8,128)(2,1)S(1)} %get-tuple-element.65), channel_id=1, source_target_pairs={{0,8},{1,9},{2,10},{3,11},{4,12},{5,13},{6,14},{7,15},{8,16},{9,17... | collective-permute-start | bytes 350216 | tf_op jit(solution)/shard_map/ppermute | solution.py:50
  200.4 18.4 %collective-permute-start.37 = (bf16[304,384]{1,0:T(8,128)(2,1)S(1)}, bf16[304,384]{1,0:T(8,128)(2,1)S(1)}, u32[]{:S(2)}, u32[]{:S(2)}) collective-permute-start(bf16[304,384]{1,0:T(8,128)(2,1)S(1)} %pad_maximum_fusion.7), channel_id=1, source_target_pairs={{0,56},{1,57},{2,58},{3,59},{4,60},{5,61},{6,62},{7,63},{8,0},{9,1... | collective-permute-start | bytes 700424 | tf_op jit(solution)/shard_map/ppermute | solution.py:50
  203.2 15.7 %collective-permute-start.33 = (bf16[304,384]{1,0:T(8,128)(2,1)S(1)}, bf16[304,384]{1,0:T(8,128)(2,1)S(1)}, u32[]{:S(2)}, u32[]{:S(2)}) collective-permute-start(bf16[304,384]{1,0:T(8,128)(2,1)S(1)} %pad_maximum_fusion.6), channel_id=1, source_target_pairs={{0,8},{1,9},{2,10},{3,11},{4,12},{5,13},{6,14},{7,15},{8,16},{9,17... | collective-permute-start | bytes 700424 | tf_op jit(solution)/shard_map/ppermute | solution.py:50
  234.7 9.9 %collective-permute-start.40 = (bf16[2,128,384]{2,1,0:T(8,128)(2,1)S(1)}, bf16[2,128,384]{2,1,0:T(8,128)(2,1)S(1)}, u32[]{:S(2)}, u32[]{:S(2)}) collective-permute-start(bf16[2,128,384]{2,1,0:T(8,128)(2,1)S(1)} %broadcast_select_fusion.3), channel_id=1, source_target_pairs={{0,1},{1,0},{2,3},{3,2},{4,5},{5,4},{6,7},{7,6},{8,9},{9,8},{10,11... | collective-permute-start | bytes 589832 | tf_op jit(solution)/shard_map/ppermute | solution.py:61
  (28 other events, 216.7 us)
Sparse Core Ops, SparseCore 0:
  10.8 115.2 all-gather.2
  139.8 69.0 reduce-scatter.1
where the time goes:
time: 257 us; the launch traced here: 252 us
  waiting for transfers between devices  100 us (39%)
  starting transfers between devices  80.8 us (31%)
  Pallas kernels  27.3 us (11%)
  local copies, waits for them, and re-layouts  15.7 us (6%)
  between operations  14.8 us (6%)
  other arithmetic  13.6 us (5%)
    ppermute x31, waiting for transfers between devices, move(): return lax.ppermute(value, 'ctx', along(axis, shift))  70.2 us
    ppermute x31, starting transfers between devices, move(): return lax.ppermute(value, 'ctx', along(axis, shift))  50 us
    ppermute x6, starting transfers between devices, swap_cores(): lax.ppermute(value, 'ctx', [(i, i ^ 1) for i in range(CHIPS * CORES)])  22.2 us
    pallas_call x2, Pallas kernels, call(): pl.pallas_call(functools.partial(attention_kernel, mine), grid_spec=pltpu...  22.1 us
    all_gather x1, waiting for transfers between devices, body(): lax.all_gather(jnp.stack([jnp.concatenate([lanes(w, p, 0), lanes(w, p, 1)...  18.9 us
    unnamed x24, local copies, waits for them, and re-layouts  6.78 us
    ppermute x1, starting transfers between devices, body(): before = lax.ppermute(tail, 'ctx', [(i, i + 1) for i in range(ends)])  5.45 us
    pallas_call x1, Pallas kernels, convolve(): pl.pallas_call(conv_kernel, grid=(channels // LANES,), in_specs=[block(fr...  5.18 us
  transfers between devices with their start and end apart: 43, of which 23 were waited for; matrix products, arithmetic and copies ran while one was open for 9% of the time, Pallas kernels for 5%

commit v1 on v0

--- a/solution.py
+++ b/solution.py
@@ -466,10 +466,13 @@
         return jnp.concatenate([jnp.where(flip, other, own), jnp.where(flip, own, other)], axis=2)
 
     early = jnp.stack([attended, query_grad])
-    early = whole(early[:, :frames], early[:, frames:])
     late = jnp.stack([key_total, value_total])
     lower, upper = late[:, :frames], late[:, frames:]
-    late = whole(jnp.where(flip, upper, lower), jnp.where(flip, lower, upper))
+    outputs = whole(
+        jnp.concatenate([early[:, :frames], jnp.where(flip, upper, lower)]),
+        jnp.concatenate([early[:, frames:], jnp.where(flip, lower, upper)]),
+    )
+    early, late = outputs[:2], outputs[2:]
     return (
         early[0][None],
         early[1][None],

time: 257 us -> 257 us (level)
  waiting for transfers between devices: 100 us -> 103 us
    ppermute x31, waiting for transfers between devices: 70.2 us -> 72.8 us  [move(): return lax.ppermute(value, 'ctx', along(axis, shift))]
    ppermute x6 -> x5, starting transfers between devices: 22.2 us -> 20.3 us  [swap_cores(): lax.ppermute(value, 'ctx', [(i, i ^ 1) for i in range(CHIPS * CORES)])]
  transfers between devices with their start and end apart: 43 -> 42, of which waited for: 23 -> 22; matrix products, arithmetic and copies ran while one was open for 9% -> 8% of each run, Pallas kernels for 5% -> 5%
where the time goes in v1:
time: 257 us; the launch traced here: 253 us
  waiting for transfers between devices  103 us (40%)
  starting transfers between devices  78.9 us (31%)
  Pallas kernels  27.4 us (11%)
  local copies, waits for them, and re-layouts  15.7 us (6%)
  between operations  14.8 us (6%)
  other arithmetic  13 us (5%)
    ppermute x31, waiting for transfers between devices, move(): return lax.ppermute(value, 'ctx', along(axis, shift))  72.8 us
    ppermute x31, starting transfers between devices, move(): return lax.ppermute(value, 'ctx', along(axis, shift))  49.9 us
    pallas_call x2, Pallas kernels, call(): pl.pallas_call(functools.partial(attention_kernel, mine), grid_spec=pltpu...  22.2 us
    ppermute x5, starting transfers between devices, swap_cores(): lax.ppermute(value, 'ctx', [(i, i ^ 1) for i in range(CHIPS * CORES)])  20.3 us
    all_gather x1, waiting for transfers between devices, body(): lax.all_gather(jnp.stack([jnp.concatenate([lanes(w, p, 0), lanes(w, p, 1)...  18.8 us
    unnamed x24, local copies, waits for them, and re-layouts  6.82 us
    ppermute x1, starting transfers between devices, body(): before = lax.ppermute(tail, 'ctx', [(i, i + 1) for i in range(ends)])  5.45 us
    pallas_call x1, Pallas kernels, convolve(): pl.pallas_call(conv_kernel, grid=(channels // LANES,), in_specs=[block(fr...  5.18 us
  transfers between devices with their start and end apart: 42, of which 22 were waited for; matrix products, arithmetic and copies ran while one was open for 8% of the time, Pallas kernels for 5%

profile of v1, /device:TPU:25, one launch (start us, length us, event | category | flops | bytes accessed | tf_op | source)
XLA Modules:
  0.0 252.9 jit_solution(4148865729319223649)
XLA Ops:
  13.3 4.0 %collective-permute-start.8 = (bf16[1,2,2,128,128]{4,3,2,1,0:T(8,128)(2,1)S(1)}, bf16[1,2,2,128,128]{4,3,2,1,0:T(8,128)(2,1)S(1)}, u32[]{:S(2)}, u32[]{:S(2)}) collective-permute-start(bf16[1,2,2,128,128]{4,3,2,1,0:T(8,128)(2,1)S(1)} %maximum_bitcast_fusion), channel_id=1, source_target_pairs={{0,56},{1,57},{2,58},{3,59},{4,60},{5,61},{6,62},{7,63},{8,0},{9,1... | collective-permute-start | bytes 393224 | tf_op jit(solution)/shard_map/ppermute | solution.py:50
  17.3 3.5 %collective-permute-done.11 = bf16[1,2,2,128,128]{4,3,2,1,0:T(8,128)(2,1)S(1)} collective-permute-done((bf16[1,2,2,128,128]{4,3,2,1,0:T(8,128)(2,1)S(1)}, bf16[1,2,2,128,128]{4,3,2,1,0:T(8,128)(2,1)S(1)}, u32[]{:S(2)}, u32[]{:S(2)}) %collective-permute-start.11) | collective-permute-done | bytes 131104 | tf_op jit(solution)/shard_map/ppermute | solution.py:50
  30.2 2.8 %collective-permute-done.13 = bf16[1,2,2,128,128]{4,3,2,1,0:T(8,128)(2,1)S(1)} collective-permute-done((bf16[1,2,2,128,128]{4,3,2,1,0:T(8,128)(2,1)S(1)}, bf16[1,2,2,128,128]{4,3,2,1,0:T(8,128)(2,1)S(1)}, u32[]{:S(2)}, u32[]{:S(2)}) %collective-permute-start.13) | collective-permute-done | bytes 131104 | tf_op jit(solution)/shard_map/ppermute | solution.py:50
  33.0 2.7 %collective-permute-start.15 = (bf16[1,2,1,128,128]{4,3,2,1,0:T(8,128)(2,1)S(1)}, bf16[1,2,1,128,128]{4,3,2,1,0:T(8,128)(2,1)S(1)}, u32[]{:S(2)}, u32[]{:S(2)}) collective-permute-start(bf16[1,2,1,128,128]{4,3,2,1,0:T(8,128)(2,1)S(1)} %slice.316), channel_id=1, source_target_pairs={{0,56},{1,57},{2,58},{3,59},{4,60},{5,61},{6,62},{7,63},{8,0},{9,1... | collective-permute-start | bytes 196616 | tf_op jit(solution)/shard_map/ppermute | solution.py:50
  44.1 5.4 %collective-permute-start.2 = (bf16[48,768]{1,0:T(8,128)(2,1)S(1)}, bf16[48,768]{1,0:T(8,128)(2,1)S(1)}, u32[]{:S(2)}, u32[]{:S(2)}) collective-permute-start(bf16[48,768]{1,0:T(8,128)(2,1)S(1)} %pad_maximum_fusion.12), channel_id=1, source_target_pairs={{0,1},{1,2},{2,3},{3,4},{4,5},{5,6},{6,7},{7,8},{8,9},{9,10},{10,1... | collective-permute-start | bytes 221192 | tf_op jit(solution)/shard_map/ppermute | solution.py:435
  51.6 12.7 %collective-permute-done.17.refs_4_ = bf16[8,2,2,128,128]{4,3,2,1,0:T(8,128)(2,1)S(1)} collective-permute-done((bf16[8,2,2,128,128]{4,3,2,1,0:T(8,128)(2,1)}, bf16[8,2,2,128,128]{4,3,2,1,0:T(8,128)(2,1)S(1)}, u32[]{:S(2)}, u32[]{:S(2)}) %collective-permute-start.17) | collective-permute-done | bytes 1048608 | tf_op jit(solution)/shard_map/ppermute | solution.py:50
  66.6 2.7 %collective-permute-start.19 = (bf16[4,2,2,128,128]{4,3,2,1,0:T(8,128)(2,1)S(1)}, bf16[4,2,2,128,128]{4,3,2,1,0:T(8,128)(2,1)S(1)}, u32[]{:S(2)}, u32[]{:S(2)}) collective-permute-start(bf16[4,2,2,128,128]{4,3,2,1,0:T(8,128)(2,1)S(1)} %slice.318), channel_id=1, source_target_pairs={{0,6},{1,7},{2,0},{3,1},{4,2},{5,3},{6,4},{7,5},{8,14},{9,15},{10,... | collective-permute-start | bytes 1572872 | tf_op jit(solution)/shard_map/ppermute | solution.py:50
  69.4 9.5 %collective-permute-start.1 = (bf16[2,128,384]{2,1,0:T(8,128)(2,1)S(1)}, bf16[2,128,384]{2,1,0:T(8,128)(2,1)S(1)}, u32[]{:S(2)}, u32[]{:S(2)}) collective-permute-start(bf16[2,128,384]{2,1,0:T(8,128)(2,1)S(1)} %get-tuple-element.82), channel_id=1, source_target_pairs={{0,1},{1,0},{2,3},{3,2},{4,5},{5,4},{6,7},{7,6},{8,9},{9,8},{10,11... | collective-permute-start | bytes 589832 | tf_op jit(solution)/shard_map/ppermute | solution.py:61
  79.5 5.2 %conv.1 = (bf16[128,768]{1,0:T(8,128)(2,1)}, bf16[128,768]{1,0:T(8,128)(2,1)}, f32[32,768]{1,0:T(8,128)}) custom-call(bf16[128,768]{1,0:T(8,128)(2,1)} %bitcast.174, bf16[128,768]{1,0:T(8,128)(2,1)} %bitcast.175, bf16[48,768]{1,0:T(8,128)(2,1)} %copy-done.6, bf16[48,768]{1,0:T(8,128)(2,1)} %copy-done.7, f32[31,768]{1,0:T(8,128)} %w_ref.1), custom_call_target="tpu_custom_call" | custom-call | flops 20000000 | bytes 1000000 | tf_op jit(solution)/shard_map/conv/pallas_call | solution.py:373
  87.4 4.2 %collective-permute-done.5 = f32[32,768]{1,0:T(8,128)S(1)} collective-permute-done((f32[32,768]{1,0:T(8,128)S(1)}, f32[32,768]{1,0:T(8,128)S(1)}, u32[]{:S(2)}, u32[]{:S(2)}) %collective-permute-start.5) | collective-permute-done | bytes 98336 | tf_op jit(solution)/shard_map/ppermute | solution.py:440
  92.6 4.1 %collective-permute-done.6 = f32[32,768]{1,0:T(8,128)S(1)} collective-permute-done((f32[32,768]{1,0:T(8,128)S(1)}, f32[32,768]{1,0:T(8,128)S(1)}, u32[]{:S(2)}, u32[]{:S(2)}) %collective-permute-start.6) | collective-permute-done | bytes 98336 | tf_op jit(solution)/shard_map/ppermute | solution.py:441
  98.6 8.6 %attend.2 = (bf16[256,384]{1,0:T(8,128)(2,1)S(1)}, bf16[256,384]{1,0:T(8,128)(2,1)S(1)}, bf16[32,224,384]{2,1,0:T(8,128)(2,1)}, bf16[32,304,384]{2,1,0:T(8,128)(...) custom-call(s32[4,16]{1,0:T(4,128)S(1)} %get-tuple-element.103.slots, ...), custom_call_target="tpu_custom_call" | custom-call | flops 1600000000 | bytes 9000000 | tf_op jit(solution)/shard_map/attend/pallas_call | solution.py:306
  107.2 18.8 %all-gather.3.cloned.1.call-done = bf16[256,128,256]{2,1,0:T(8,128)(2,1)} async-done(((bf16[4,128,256]{2,1,0:T(8,128)(2,1)}), bf16[256,128,256]{2,1,0:T(8,128)(2,1)}) %all-gather.3.cloned.1.call-update) | async-done | bytes 16777232 | tf_op jit(solution)/shard_map/all_gather | solution.py:403
  126.0 13.6 %attend.3 = (bf16[256,384]{1,0:T(8,128)(2,1)S(1)}, bf16[256,384]{1,0:T(8,128)(2,1)S(1)}, bf16[32,224,384]{2,1,0:T(8,128)(2,1)}, bf16[32,304,384]{2,1,0:T(8,128)(...) custom-call(s32[4,16]{1,0:T(4,128)S(1)} %get-tuple-element.103.slots, ...), custom_call_target="tpu_custom_call", output_to_operand_aliasing={{0}: (8, {}), {1}: (9, {}), {2}: (10, {}), {3}: (11, {}), {... | custom-call | flops 3200000000 | bytes 18000000 | tf_op jit(solution)/shard_map/attend/pallas_call | solution.py:306
  140.7 10.4 %collective-permute-start.25 = (bf16[2,304,384]{2,1,0:T(8,128)(2,1)S(1)}, bf16[2,304,384]{2,1,0:T(8,128)(2,1)S(1)}, u32[]{:S(2)}, u32[]{:S(2)}) collective-permute-start(bf16[2,304,384]{2,1,0:T(8,128)(2,1)S(1)} %get-tuple-element.42), channel_id=1, source_target_pairs={{0,6},{1,7},{2,0},{3,1},{4,2},{5,3},{6,4},{7,5},{8,14},{9,15},{10,... | collective-permute-start | bytes 1400840 | tf_op jit(solution)/shard_map/ppermute | solution.py:50
  156.1 5.2 %collective-permute-done.25 = bf16[2,304,384]{2,1,0:T(8,128)(2,1)S(1)} collective-permute-done((bf16[2,304,384]{2,1,0:T(8,128)(2,1)S(1)}, bf16[2,304,384]{2,1,0:T(8,128)(2,1)S(1)}, u32[]{:S(2)}, u32[]{:S(2)}) %collective-permute-start.25) | collective-permute-done | bytes 466976 | tf_op jit(solution)/shard_map/ppermute | solution.py:50
  161.3 10.0 %collective-permute-done.29 = bf16[2,304,384]{2,1,0:T(8,128)(2,1)S(1)} collective-permute-done((bf16[2,304,384]{2,1,0:T(8,128)(2,1)S(1)}, bf16[2,304,384]{2,1,0:T(8,128)(2,1)S(1)}, u32[]{:S(2)}, u32[]{:S(2)}) %collective-permute-start.29) | collective-permute-done | bytes 466976 | tf_op jit(solution)/shard_map/ppermute | solution.py:50
  172.8 3.0 %collective-permute-start.30 = (bf16[3,304,384]{2,1,0:T(8,128)(2,1)S(1)}, bf16[3,304,384]{2,1,0:T(8,128)(2,1)S(1)}, u32[]{:S(2)}, u32[]{:S(2)}) collective-permute-start(bf16[3,304,384]{2,1,0:T(8,128)(2,1)S(1)} %pad_maximum_fusion.3), channel_id=1, source_target_pairs={{0,6},{1,7},{2,0},{3,1},{4,2},{5,3},{6,4},{7,5},{8,14},{9,15},{10,... | collective-permute-start | bytes 2101256 | tf_op jit(solution)/shard_map/ppermute | solution.py:50
  177.2 9.3 %collective-permute-done.28 = bf16[3,304,384]{2,1,0:T(8,128)(2,1)S(1)} collective-permute-done((bf16[3,304,384]{2,1,0:T(8,128)(2,1)S(1)}, bf16[3,304,384]{2,1,0:T(8,128)(2,1)S(1)}, u32[]{:S(2)}, u32[]{:S(2)}) %collective-permute-start.28) | collective-permute-done | bytes 700448 | tf_op jit(solution)/shard_map/ppermute | solution.py:50
  186.5 2.9 %collective-permute-done.30 = bf16[3,304,384]{2,1,0:T(8,128)(2,1)S(1)} collective-permute-done((bf16[3,304,384]{2,1,0:T(8,128)(2,1)S(1)}, bf16[3,304,384]{2,1,0:T(8,128)(2,1)S(1)}, u32[]{:S(2)}, u32[]{:S(2)}) %collective-permute-start.30) | collective-permute-done | bytes 700448 | tf_op jit(solution)/shard_map/ppermute | solution.py:50
  195.1 5.2 %collective-permute-done.31 = bf16[152,384]{1,0:T(8,128)(2,1)S(1)} collective-permute-done((bf16[152,384]{1,0:T(8,128)(2,1)S(1)}, bf16[152,384]{1,0:T(8,128)(2,1)S(1)}, u32[]{:S(2)}, u32[]{:S(2)}) %collective-permute-start.31) | collective-permute-done | bytes 116768 | tf_op jit(solution)/shard_map/ppermute | solution.py:50
  200.4 2.7 %collective-permute-start.36 = (bf16[304,384]{1,0:T(8,128)(2,1)S(1)}, bf16[304,384]{1,0:T(8,128)(2,1)S(1)}, u32[]{:S(2)}, u32[]{:S(2)}) collective-permute-start(bf16[304,384]{1,0:T(8,128)(2,1)S(1)} %pad_maximum_fusion.9), channel_id=1, source_target_pairs={{0,56},{1,57},{2,58},{3,59},{4,60},{5,61},{6,62},{7,63},{8,0},{9,1... | collective-permute-start | bytes 700424 | tf_op jit(solution)/shard_map/ppermute | solution.py:50
  203.3 11.2 %collective-permute-done.26 = bf16[5,304,384]{2,1,0:T(8,128)(2,1)S(1)} collective-permute-done((bf16[5,304,384]{2,1,0:T(8,128)(2,1)S(1)}, bf16[5,304,384]{2,1,0:T(8,128)(2,1)S(1)}, u32[]{:S(2)}, u32[]{:S(2)}) %collective-permute-start.26) | collective-permute-done | bytes 1167392 | tf_op jit(solution)/shard_map/ppermute | solution.py:50
  234.8 8.6 %collective-permute-start.39 = (bf16[4,128,384]{2,1,0:T(8,128)(2,1)S(1)}, bf16[4,128,384]{2,1,0:T(8,128)(2,1)S(1)}, u32[]{:S(2)}, u32[]{:S(2)}) collective-permute-start(bf16[4,128,384]{2,1,0:T(8,128)(2,1)S(1)} %pad_maximum_fusion.6), channel_id=1, source_target_pairs={{0,1},{1,0},{2,3},{3,2},{4,5},{5,4},{6,7},{7,6},{8,9},{9,8},{10,11... | collective-permute-start | bytes 1179656 | tf_op jit(solution)/shard_map/ppermute | solution.py:61
  (146 shorter events, 71.6 us)
Async XLA Ops:
  7.2 118.9 %all-gather.3.cloned.1.call-start = ((), (), s32[]{:S(2)}) async-start(), calls=%async_computation.2 | async-start | bytes 17039360 | tf_op jit(solution)/shard_map/all_gather | solution.py:403
  9.8 212.0 %reduce-scatter.2.cloned.1.call-start = ((), (), s32[]{:S(2)}) async-start(), calls=%async_computation.1 | async-start | bytes 6193152 | tf_op jit(solution)/shard_map/reduce_scatter | solution.py:449
  11.6 9.2 %collective-permute-start.11 = (bf16[1,2,2,128,128]{4,3,2,1,0:T(8,128)(2,1)S(1)}, bf16[1,2,2,128,128]{4,3,2,1,0:T(8,128)(2,1)S(1)}, u32[]{:S(2)}, u32[]{:S(2)}) collective-permute-start(bf16[1,2,2,128,128]{4,3,2,1,0:T(8,128)(2,1)S(1)} %maximum_bitcast_fusion), channel_id=1, source_target_pairs={{0,8},{1,9},{2,10},{3,11},{4,12},{5,13},{6,14},{7,15},{8,16},{9,17... | collective-permute-start | bytes 393224 | tf_op jit(solution)/shard_map/ppermute | solution.py:50
  23.5 61.2 %collective-permute-start = (s32[2,16]{1,0:T(2,128)S(1)}, s32[2,16]{1,0:T(2,128)S(1)}, u32[]{:S(2)}, u32[]{:S(2)}) collective-permute-start(s32[2,16]{1,0:T(2,128)S(1)} %bitcast.176), channel_id=1, source_target_pairs={{0,1},{1,0},{2,3},{3,2},{4,5},{5,4},{6,7},{7,6},{8,9},{9,8},{10,11... | collective-permute-start | bytes 392 | tf_op jit(solution)/shard_map/ppermute | solution.py:61
  40.3 24.1 %collective-permute-start.17 = (bf16[8,2,2,128,128]{4,3,2,1,0:T(8,128)(2,1)}, bf16[8,2,2,128,128]{4,3,2,1,0:T(8,128)(2,1)S(1)}, u32[]{:S(2)}, u32[]{:S(2)}) collective-permute-start(bf16[8,2,2,128,128]{4,3,2,1,0:T(8,128)(2,1)} %constant_dynamic-update-slice_fusion.2.refs_0_), channel_id=1, source_target_pairs={{0,2},{1,3},{2,4},{3,5},{4,6},{5,7},{6,0},{7,1},{8,10},{9,11},{10,... | collective-permute-start | bytes 3145736 | tf_op jit(solution)/shard_map/ppermute | solution.py:50
  41.7 23.7 %collective-permute-start.16 = (bf16[8,2,2,128,128]{4,3,2,1,0:T(8,128)(2,1)}, bf16[8,2,2,128,128]{4,3,2,1,0:T(8,128)(2,1)}, u32[]{:S(2)}, u32[]{:S(2)}) collective-permute-start(bf16[8,2,2,128,128]{4,3,2,1,0:T(8,128)(2,1)} %constant_dynamic-update-slice_fusion.2.refs_0_), channel_id=1, source_target_pairs={{0,6},{1,7},{2,0},{3,1},{4,2},{5,3},{6,4},{7,5},{8,14},{9,15},{10,... | collective-permute-start | bytes 3145736 | tf_op jit(solution)/shard_map/ppermute | solution.py:50
  44.1 25.3 %collective-permute-start.2 = (bf16[48,768]{1,0:T(8,128)(2,1)S(1)}, bf16[48,768]{1,0:T(8,128)(2,1)S(1)}, u32[]{:S(2)}, u32[]{:S(2)}) collective-permute-start(bf16[48,768]{1,0:T(8,128)(2,1)S(1)} %pad_maximum_fusion.12), channel_id=1, source_target_pairs={{0,1},{1,2},{2,3},{3,4},{4,5},{5,6},{6,7},{7,8},{8,9},{9,10},{10,1... | collective-permute-start | bytes 221192 | tf_op jit(solution)/shard_map/ppermute | solution.py:435
  49.5 29.3 %collective-permute-start.3 = (bf16[48,768]{1,0:T(8,128)(2,1)S(1)}, bf16[48,768]{1,0:T(8,128)(2,1)S(1)}, u32[]{:S(2)}, u32[]{:S(2)}) collective-permute-start(bf16[48,768]{1,0:T(8,128)(2,1)S(1)} %pad_maximum_fusion.13), channel_id=1, source_target_pairs={{1,0},{2,1},{3,2},{4,3},{5,4},{6,5},{7,6},{8,7},{9,8},{10,9},{11,1... | collective-permute-start | bytes 221192 | tf_op jit(solution)/shard_map/ppermute | solution.py:436
  65.4 31.3 %collective-permute-start.18 = (bf16[4,2,2,128,128]{4,3,2,1,0:T(8,128)(2,1)S(1)}, bf16[4,2,2,128,128]{4,3,2,1,0:T(8,128)(2,1)S(1)}, u32[]{:S(2)}, u32[]{:S(2)}) collective-permute-start(bf16[4,2,2,128,128]{4,3,2,1,0:T(8,128)(2,1)S(1)} %slice.317), channel_id=1, source_target_pairs={{0,2},{1,3},{2,4},{3,5},{4,6},{5,7},{6,0},{7,1},{8,10},{9,11},{10,... | collective-permute-start | bytes 1572872 | tf_op jit(solution)/shard_map/ppermute | solution.py:50
  66.6 30.1 %collective-permute-start.19 = (bf16[4,2,2,128,128]{4,3,2,1,0:T(8,128)(2,1)S(1)}, bf16[4,2,2,128,128]{4,3,2,1,0:T(8,128)(2,1)S(1)}, u32[]{:S(2)}, u32[]{:S(2)}) collective-permute-start(bf16[4,2,2,128,128]{4,3,2,1,0:T(8,128)(2,1)S(1)} %slice.318), channel_id=1, source_target_pairs={{0,6},{1,7},{2,0},{3,1},{4,2},{5,3},{6,4},{7,5},{8,14},{9,15},{10,... | collective-permute-start | bytes 1572872 | tf_op jit(solution)/shard_map/ppermute | solution.py:50
  69.4 23.1 %collective-permute-start.1 = (bf16[2,128,384]{2,1,0:T(8,128)(2,1)S(1)}, bf16[2,128,384]{2,1,0:T(8,128)(2,1)S(1)}, u32[]{:S(2)}, u32[]{:S(2)}) collective-permute-start(bf16[2,128,384]{2,1,0:T(8,128)(2,1)S(1)} %get-tuple-element.82), channel_id=1, source_target_pairs={{0,1},{1,0},{2,3},{3,2},{4,5},{5,4},{6,7},{7,6},{8,9},{9,8},{10,11... | collective-permute-start | bytes 589832 | tf_op jit(solution)/shard_map/ppermute | solution.py:61
  139.7 15.2 %collective-permute-start.27 = (bf16[1,304,384]{2,1,0:T(8,128)(2,1)S(1)}, bf16[1,304,384]{2,1,0:T(8,128)(2,1)S(1)}, u32[]{:S(2)}, u32[]{:S(2)}) collective-permute-start(bf16[1,304,384]{2,1,0:T(8,128)(2,1)S(1)} %get-tuple-element.43), channel_id=1, source_target_pairs={{0,2},{1,3},{2,4},{3,5},{4,6},{5,7},{6,0},{7,1},{8,10},{9,11},{10,... | collective-permute-start | bytes 700424 | tf_op jit(solution)/shard_map/ppermute | solution.py:50
  140.7 20.5 %collective-permute-start.25 = (bf16[2,304,384]{2,1,0:T(8,128)(2,1)S(1)}, bf16[2,304,384]{2,1,0:T(8,128)(2,1)S(1)}, u32[]{:S(2)}, u32[]{:S(2)}) collective-permute-start(bf16[2,304,384]{2,1,0:T(8,128)(2,1)S(1)} %get-tuple-element.42), channel_id=1, source_target_pairs={{0,6},{1,7},{2,0},{3,1},{4,2},{5,3},{6,4},{7,5},{8,14},{9,15},{10,... | collective-permute-start | bytes 1400840 | tf_op jit(solution)/shard_map/ppermute | solution.py:50
  151.1 20.2 %collective-permute-start.29 = (bf16[2,304,384]{2,1,0:T(8,128)(2,1)S(1)}, bf16[2,304,384]{2,1,0:T(8,128)(2,1)S(1)}, u32[]{:S(2)}, u32[]{:S(2)}) collective-permute-start(bf16[2,304,384]{2,1,0:T(8,128)(2,1)S(1)} %get-tuple-element.44), channel_id=1, source_target_pairs={{0,6},{1,7},{2,0},{3,1},{4,2},{5,3},{6,4},{7,5},{8,14},{9,15},{10,... | collective-permute-start | bytes 1400840 | tf_op jit(solution)/shard_map/ppermute | solution.py:50
  154.0 23.2 %collective-permute-start.23 = (bf16[3,304,384]{2,1,0:T(8,128)(2,1)S(1)}, bf16[3,304,384]{2,1,0:T(8,128)(2,1)S(1)}, u32[]{:S(2)}, u32[]{:S(2)}) collective-permute-start(bf16[3,304,384]{2,1,0:T(8,128)(2,1)S(1)} %get-tuple-element.41), channel_id=1, source_target_pairs={{0,2},{1,3},{2,4},{3,5},{4,6},{5,7},{6,0},{7,1},{8,10},{9,11},{10,... | collective-permute-start | bytes 2101256 | tf_op jit(solution)/shard_map/ppermute | solution.py:50
  156.0 30.5 %collective-permute-start.28 = (bf16[3,304,384]{2,1,0:T(8,128)(2,1)S(1)}, bf16[3,304,384]{2,1,0:T(8,128)(2,1)S(1)}, u32[]{:S(2)}, u32[]{:S(2)}) collective-permute-start(bf16[3,304,384]{2,1,0:T(8,128)(2,1)S(1)} %pad_maximum_fusion.2), channel_id=1, source_target_pairs={{0,2},{1,3},{2,4},{3,5},{4,6},{5,7},{6,0},{7,1},{8,10},{9,11},{10,... | collective-permute-start | bytes 2101256 | tf_op jit(solution)/shard_map/ppermute | solution.py:50
  172.8 16.7 %collective-permute-start.30 = (bf16[3,304,384]{2,1,0:T(8,128)(2,1)S(1)}, bf16[3,304,384]{2,1,0:T(8,128)(2,1)S(1)}, u32[]{:S(2)}, u32[]{:S(2)}) collective-permute-start(bf16[3,304,384]{2,1,0:T(8,128)(2,1)S(1)} %pad_maximum_fusion.3), channel_id=1, source_target_pairs={{0,6},{1,7},{2,0},{3,1},{4,2},{5,3},{6,4},{7,5},{8,14},{9,15},{10,... | collective-permute-start | bytes 2101256 | tf_op jit(solution)/shard_map/ppermute | solution.py:50
  177.1 37.4 %collective-permute-start.26 = (bf16[5,304,384]{2,1,0:T(8,128)(2,1)S(1)}, bf16[5,304,384]{2,1,0:T(8,128)(2,1)S(1)}, u32[]{:S(2)}, u32[]{:S(2)}) collective-permute-start(bf16[5,304,384]{2,1,0:T(8,128)(2,1)S(1)} %pad_maximum_fusion.1), channel_id=1, source_target_pairs={{0,6},{1,7},{2,0},{3,1},{4,2},{5,3},{6,4},{7,5},{8,14},{9,15},{10,... | collective-permute-start | bytes 3502088 | tf_op jit(solution)/shard_map/ppermute | solution.py:50
  191.4 25.7 %collective-permute-start.24 = (bf16[5,304,384]{2,1,0:T(8,128)(2,1)S(1)}, bf16[5,304,384]{2,1,0:T(8,128)(2,1)S(1)}, u32[]{:S(2)}, u32[]{:S(2)}) collective-permute-start(bf16[5,304,384]{2,1,0:T(8,128)(2,1)S(1)} %pad_maximum_fusion), channel_id=1, source_target_pairs={{0,2},{1,3},{2,4},{3,5},{4,6},{5,7},{6,0},{7,1},{8,10},{9,11},{10,... | collective-permute-start | bytes 3502088 | tf_op jit(solution)/shard_map/ppermute | solution.py:50
  192.3 8.0 %collective-permute-start.31 = (bf16[152,384]{1,0:T(8,128)(2,1)S(1)}, bf16[152,384]{1,0:T(8,128)(2,1)S(1)}, u32[]{:S(2)}, u32[]{:S(2)}) collective-permute-start(bf16[152,384]{1,0:T(8,128)(2,1)S(1)} %get-tuple-element.71), channel_id=1, source_target_pairs={{0,8},{1,9},{2,10},{3,11},{4,12},{5,13},{6,14},{7,15},{8,16},{9,17... | collective-permute-start | bytes 350216 | tf_op jit(solution)/shard_map/ppermute | solution.py:50
  192.4 7.9 %collective-permute-start.35 = (bf16[152,384]{1,0:T(8,128)(2,1)S(1)}, bf16[152,384]{1,0:T(8,128)(2,1)S(1)}, u32[]{:S(2)}, u32[]{:S(2)}) collective-permute-start(bf16[152,384]{1,0:T(8,128)(2,1)S(1)} %get-tuple-element.72), channel_id=1, source_target_pairs={{0,56},{1,57},{2,58},{3,59},{4,60},{5,61},{6,62},{7,63},{8,0},{9,1... | collective-permute-start | bytes 350216 | tf_op jit(solution)/shard_map/ppermute | solution.py:50
  200.4 18.4 %collective-permute-start.36 = (bf16[304,384]{1,0:T(8,128)(2,1)S(1)}, bf16[304,384]{1,0:T(8,128)(2,1)S(1)}, u32[]{:S(2)}, u32[]{:S(2)}) collective-permute-start(bf16[304,384]{1,0:T(8,128)(2,1)S(1)} %pad_maximum_fusion.9), channel_id=1, source_target_pairs={{0,56},{1,57},{2,58},{3,59},{4,60},{5,61},{6,62},{7,63},{8,0},{9,1... | collective-permute-start | bytes 700424 | tf_op jit(solution)/shard_map/ppermute | solution.py:50
  203.2 15.7 %collective-permute-start.32 = (bf16[304,384]{1,0:T(8,128)(2,1)S(1)}, bf16[304,384]{1,0:T(8,128)(2,1)S(1)}, u32[]{:S(2)}, u32[]{:S(2)}) collective-permute-start(bf16[304,384]{1,0:T(8,128)(2,1)S(1)} %pad_maximum_fusion.8), channel_id=1, source_target_pairs={{0,8},{1,9},{2,10},{3,11},{4,12},{5,13},{6,14},{7,15},{8,16},{9,17... | collective-permute-start | bytes 700424 | tf_op jit(solution)/shard_map/ppermute | solution.py:50
  234.8 10.0 %collective-permute-start.39 = (bf16[4,128,384]{2,1,0:T(8,128)(2,1)S(1)}, bf16[4,128,384]{2,1,0:T(8,128)(2,1)S(1)}, u32[]{:S(2)}, u32[]{:S(2)}) collective-permute-start(bf16[4,128,384]{2,1,0:T(8,128)(2,1)S(1)} %pad_maximum_fusion.6), channel_id=1, source_target_pairs={{0,1},{1,0},{2,3},{3,2},{4,5},{5,4},{6,7},{7,6},{8,9},{9,8},{10,11... | collective-permute-start | bytes 1179656 | tf_op jit(solution)/shard_map/ppermute | solution.py:61
  (27 other events, 209.1 us)
Sparse Core Ops, SparseCore 0:
  10.8 115.2 all-gather.2
  139.8 69.0 reduce-scatter.1
